TPU v7x, 32 devices: a whole 2x2x4 slice. The times are simulated.
32 devices in a mesh: rec: 4 (over z), tm: 8 (over y, x, core).
Axes of the slice: x: 2, y: 2, z: 4, core: 2. Of those that a mesh axis runs over, the one named last changes fastest.
Arguments:
- audio: float32 [4, 40960], P('rec', 'tm'), may hold values from -100 to 100, as said below
- conv0_weight: float32 [10, 512], replicated, may hold values from -2 to 2
- norm_gain: float32 [512], replicated, may hold values from 0.25 to 1.75
- norm_bias: float32 [512], replicated, may hold values from -3 to 3
- conv1_weight: bfloat16 [1536, 512], replicated, may hold values from -0.25 to 0.25
- conv2_weight: bfloat16 [1536, 512], replicated, may hold values from -0.25 to 0.25
- cotangent: bfloat16 [4, 2048, 512], P('rec', 'tm'), may hold values from -0.09375 to 0.09375
Outputs:
- features: bfloat16 [4, 2048, 512], P('rec', 'tm')
- grad_conv0: float32 [10, 512], replicated
- grad_gain: float32 [512], replicated
- grad_bias: float32 [512], replicated
- grad_conv1: float32 [1536, 512], replicated
- grad_conv2: float32 [1536, 512], replicated
Inputs may be any that keep to these rules, and one draw needn't show every extreme that they name: `audio`: recorded waveforms, one row a recording.
All inputs are finite; a program needn't handle non-finite values.
Results may differ from a plain program's by a relative error of at most 0.0095.
Values may be sent and summed in bfloat16 or wider, within the bound.
A program may use at most 64 MiB of HBM per device.

v0:
```python
import functools

import jax
import jax.numpy as jnp
from jax import lax
from jax.experimental import pallas as pl
from jax.experimental.pallas import tpu as pltpu
from jax.sharding import PartitionSpec as P

EPS = 1e-05
HIGH = lax.Precision.HIGHEST
MESH = pl.DeviceIdType.MESH
F32, BF16 = jnp.float32, jnp.bfloat16
EDGE = 16
STEP = 16


def gelu_parts(value):
    phi = 0.5 * (1.0 + lax.erf(value * 0.7071067811865476))
    slope = phi + value * jnp.exp(-0.5 * value * value) * 0.3989422804014327
    return value * phi, slope


def dot(a, b, ca, cb, precision=None):
    return lax.dot_general(
        a, b, (((ca,), (cb,)), ((), ())), precision=precision, preferred_element_type=F32
    )


def plan(tm, rec):
    inner = [("tm", 1 << i) for i in range(1, tm.bit_length() - 1)]
    low, high = inner[: len(inner) // 2], inner[len(inner) // 2 :]
    outer = [("rec", 1 << i) for i in range(rec.bit_length() - 1)]
    core = [("tm", 1)]
    one, two = core + low + high + outer, core + high + low + outer
    return [one, two, core + outer + low + high, one, two, core + outer + high + low]


def kernel(
    tm, rec, audio_ref, taps_ref, gain_ref, bias_ref, w1_hbm, w2_hbm, cot_ref,
    features_ref, res_ref, small_ref,
    norm_ref, slope0_ref, act0_ref, pre1_ref, slope1_ref, act1_ref, pre2_ref, delta2_ref, delta1_ref,
    x_ref, xx_ref, wide_ref, edge_ref, dn_ref, t0_ref, t1_ref, gf_ref, sendbuf, recvbuf, stat_ref, stat_in, little, little_in,
    w1_ref, w2_ref, load_sem, ed_send, ed_recv, rs_send, rs_recv, st_send, st_recv, sm_send, sm_recv,
):
    me = {"tm": lax.axis_index("tm"), "rec": lax.axis_index("rec")}
    rows_all, channels = norm_ref.shape[0], gain_ref.shape[1]
    rows = rows_all - EDGE
    count = 4.0 * rows * tm
    orders = plan(tm, rec)
    stages, parts = len(orders[0]), len(orders)
    share_rows = gf_ref.shape[0] // parts
    C = channels

    def bit_of(stage):
        axis, bit = stage
        return lax.rem(me[axis] // bit, 2)

    def partner(stage):
        axis, bit = stage
        return {axis: me[axis] + bit * (1 - 2 * bit_of(stage))}

    loads = [
        pltpu.make_async_copy(w1_hbm, w1_ref, load_sem.at[0]),
        pltpu.make_async_copy(w2_hbm, w2_ref, load_sem.at[1]),
    ]
    for load in loads:
        load.start()
    barrier = pltpu.get_barrier_semaphore()
    rec_bits = [s for s in orders[0] if s[0] == "rec"]
    for d in range(1, tm):
        pl.semaphore_signal(barrier, inc=1, device_id={"tm": lax.rem(me["tm"] + d, tm)}, device_id_type=MESH)
    for stage in rec_bits:
        pl.semaphore_signal(barrier, inc=1, device_id=partner(stage), device_id_type=MESH)

    x_ref[:rows, :] = audio_ref[...]
    for q in range(4):
        wide = taps_ref[...] if q == 0 else pltpu.roll(taps_ref[...], 5 * q, 0)
        wide_ref[:, q * C : (q + 1) * C] = wide
    pl.semaphore_wait(barrier, tm - 1 + len(rec_bits))
    behind, ahead = lax.rem(me["tm"] + 1, tm), lax.rem(me["tm"] + tm - 1, tm)
    edges = []
    for i, (source, target, device) in enumerate((
        (x_ref.at[0:8, :], x_ref.at[rows : rows + 8, :], ahead),
        (x_ref.at[rows - 8 : rows, :], x_ref.at[rows + 8 : rows + 16, :], behind),
        (cot_ref.at[rows - 16 : rows, :], edge_ref, behind),
    )):
        copy = pltpu.make_async_remote_copy(
            src_ref=source, dst_ref=target, send_sem=ed_send.at[i], recv_sem=ed_recv.at[i],
            device_id={"tm": device}, device_id_type=MESH,
        )
        copy.start()
        edges.append(copy)
    for copy in edges[:2]:
        copy.wait()

    row = lax.broadcasted_iota(jnp.int32, x_ref.shape, 0)
    lane = lax.broadcasted_iota(jnp.int32, x_ref.shape, 1)
    outside = jnp.logical_or(
        jnp.logical_and(row >= rows + 8, me["tm"] == 0),
        jnp.logical_and(jnp.logical_and(row >= rows, row < rows + 8), me["tm"] == tm - 1),
    )
    x = jnp.where(outside, 0.0, x_ref[...])
    next_row = jnp.where(lane < 5, pltpu.roll(x, rows_all - 1, 0), 0.0)
    xx_ref[...] = x + pltpu.roll(next_row, 20, 1)
    for q in range(4):
        lanes = slice(q * C, (q + 1) * C)
        norm_ref[:, lanes] = dot(xx_ref[:, :32], wide_ref[:, lanes], 1, 0, HIGH)

    def sums(i, carry):
        one, two = carry
        for q in range(4):
            part = norm_ref[pl.ds(i * STEP, STEP), q * C : (q + 1) * C]
            one, two = one + part, two + part * part
        return one, two

    zero = jnp.zeros((STEP, C), F32)
    one, two = lax.fori_loop(0, rows // STEP, sums, (zero, zero))
    stat_ref[0, 0:1, :] = jnp.sum(one, 0, keepdims=True)
    stat_ref[0, 1:2, :] = jnp.sum(two, 0, keepdims=True)

    def share(which):
        copies = []
        for d in range(1, tm):
            copy = pltpu.make_async_remote_copy(
                src_ref=stat_ref.at[which],
                dst_ref=stat_in.at[which, d],
                send_sem=st_send.at[which, d],
                recv_sem=st_recv.at[which, d],
                device_id={"tm": lax.rem(me["tm"] + d, tm)},
                device_id_type=MESH,
            )
            copy.start()
            copies.append(copy)
        return copies

    def gathered(which, copies):
        total = stat_ref[which]
        for d, copy in enumerate(copies):
            copy.wait_recv()
            total = total + stat_in[which, d + 1]
        for copy in copies:
            copy.wait_send()
        return total

    total = gathered(0, share(0))
    mean = total[0:1] / count
    variance = total[1:2] / count - mean * mean
    inverse = lax.rsqrt(variance + EPS)
    gain, bias = gain_ref[...], bias_ref[...]

    def first_act(i, carry):
        at = pl.ds(pl.multiple_of(i * STEP, STEP), STEP)
        row = i * STEP + lax.broadcasted_iota(jnp.int32, (STEP, C), 0)
        past = jnp.logical_and(row == rows, me["tm"] == tm - 1)
        for q in range(4):
            lanes = slice(q * C, (q + 1) * C)
            normed = (norm_ref[at, lanes] - mean) * inverse
            norm_ref[at, lanes] = normed
            act, slope = gelu_parts(normed * gain + bias)
            act0_ref[at, lanes] = jnp.where(past, 0.0, act).astype(BF16)
            slope0_ref[at, lanes] = slope
        return carry

    lax.fori_loop(0, rows_all // STEP, first_act, 0)
    act0_ref[:, 4 * C :] = pltpu.roll(act0_ref[:, :C].astype(F32), rows_all - 1, 0).astype(BF16)

    loads[0].wait()
    pre1_ref[:, :C] = dot(act0_ref[:, : 3 * C], w1_ref[...], 1, 0)
    pre1_ref[:, C:] = dot(act0_ref[:, 2 * C :], w1_ref[...], 1, 0)

    def second_act(i, carry):
        at = pl.ds(pl.multiple_of(i * STEP, STEP), STEP)
        row = i * STEP + lax.broadcasted_iota(jnp.int32, (STEP, 2 * C), 0)
        past = jnp.logical_and(row == rows, me["tm"] == tm - 1)
        act, slope = gelu_parts(pre1_ref[at, :])
        act1_ref[at, : 2 * C] = jnp.where(past, 0.0, act).astype(BF16)
        slope1_ref[at, :] = slope
        return carry

    lax.fori_loop(0, rows_all // STEP, second_act, 0)
    act1_ref[:, 2 * C :] = pltpu.roll(act1_ref[:, :C].astype(F32), rows_all - 1, 0).astype(BF16)

    loads[1].wait()
    pre2_ref[...] = dot(act1_ref[...], w2_ref[...], 1, 0)

    def third_act(i, carry):
        at = pl.ds(pl.multiple_of(i * STEP, STEP), STEP)
        act, slope = gelu_parts(pre2_ref[at, :])
        features_ref[at, :] = act.astype(BF16)
        delta2_ref[at, :] = (cot_ref[at, :].astype(F32) * slope).astype(BF16)
        return carry

    lax.fori_loop(0, rows // STEP, third_act, 0)
    edges[2].wait()
    slope = gelu_parts(pre2_ref[rows:, :])[1]
    edge = jnp.where(me["tm"] == 0, 0.0, edge_ref[...].astype(F32))
    delta2_ref[rows:, :] = (edge * slope).astype(BF16)

    state = [{"size": share_rows, "start": p * share_rows, "used": 0, "step": 0, "sent": [], "back": []} for p in range(parts)]

    def combine(target, part, start, size, came_at):
        block = min(32, size)

        def body(i, carry):
            at = pl.ds(pl.multiple_of(start + i * block, 16), block)
            value = gf_ref[at, :]
            if came_at is not None:
                value = value + recvbuf[part, pl.ds(pl.multiple_of(came_at + i * block, 16), block), :].astype(F32)
            target[at, :] = value.astype(target.dtype)
            return carry

        lax.fori_loop(0, size // block, body, 0)

    def send_piece(part, ref_from, ref_to, index, stage):
        copy = pltpu.make_async_remote_copy(
            src_ref=ref_from, dst_ref=ref_to,
            send_sem=rs_send.at[part, index], recv_sem=rs_recv.at[part, index],
            device_id=partner(stage), device_id_type=MESH,
        )
        copy.start()
        return copy

    def advance(part):
        s = state[part]
        step, size, start = s["step"], s["size"], s["start"]
        s["step"] += 1
        if step <= stages:
            base = None
            if step > 0:
                last, _, _, last_half, whole = s["sent"][-1]
                last.wait_recv()
                if whole:
                    last.wait_send()
                base = s["used"] - last_half
        if step < stages:
            stage = orders[part][step]
            whole = size // 2 < 16
            if whole:
                half, keep, away = size, start, start
                if base is not None:
                    combine(gf_ref, part, start, size, base)
                combine(sendbuf, part, start, size, None)
            else:
                half, bit = size // 2, bit_of(stage)
                keep, away = start + bit * half, start + (1 - bit) * half
                combine(sendbuf, part, away, half, None if base is None else base + (1 - bit) * half)
            copy = send_piece(
                part,
                sendbuf.at[pl.ds(pl.multiple_of(away, 16), half), :],
                recvbuf.at[part, pl.ds(s["used"], half), :],
                step, stage,
            )
            if not whole and base is not None:
                combine(gf_ref, part, keep, half, base + bit * half)
            s["sent"].append((copy, keep, size, half, whole))
            s["size"], s["start"], s["used"] = half, keep, s["used"] + half
            return
        if step == stages:
            combine(res_ref, part, start, size, base)
        elif s["back"]:
            s["back"][-1].wait_recv()
        index = 2 * stages - 1 - step
        if index >= 0:
            _, keep, _, half, whole = s["sent"][index]
            if not whole:
                piece = res_ref.at[pl.ds(pl.multiple_of(keep, 16), half), :]
                s["back"].append(send_piece(part, piece, piece, stages + index, orders[part][index]))

    gf_ref[: 3 * C, :] = dot(act1_ref[:rows, :], delta2_ref[:rows, :], 0, 0)
    for part in (0, 1, 2):
        advance(part)
    t0_ref[...] = dot(delta2_ref[...], w2_ref[...], 1, 1)
    even = t0_ref[:, :C] + pltpu.roll(t0_ref[:, 2 * C :], 1, 0)
    delta1_ref[:, :C] = (even * slope1_ref[:, :C]).astype(BF16)
    delta1_ref[:, C:] = (t0_ref[:, C : 2 * C] * slope1_ref[:, C:]).astype(BF16)
    for part in (0, 1, 2):
        advance(part)

    gf_ref[3 * C :, :] = dot(act0_ref[:rows, : 3 * C], delta1_ref[:rows, :C], 0, 0)
    gf_ref[3 * C :, :] += dot(act0_ref[:rows, 2 * C :], delta1_ref[:rows, C:], 0, 0)
    for part in (3, 4, 5):
        advance(part)
    t0_ref[...] = dot(delta1_ref[:, :C], w1_ref[...], 1, 1)
    t1_ref[...] = dot(delta1_ref[:, C:], w1_ref[...], 1, 1)
    for part in (0, 3, 1, 4, 2, 5):
        advance(part)
    t1_ref[:, 2 * C :] = pltpu.roll(t1_ref[:, 2 * C :], 1, 0)

    def back(i, carry):
        one, two = carry
        at = pl.ds(pl.multiple_of(i * STEP, STEP), STEP)
        grads = (
            t0_ref[at, :C] + t1_ref[at, 2 * C :],
            t0_ref[at, C : 2 * C],
            t0_ref[at, 2 * C :] + t1_ref[at, :C],
            t1_ref[at, C : 2 * C],
        )
        for q in range(4):
            lanes = slice(q * C, (q + 1) * C)
            dnorm = grads[q] * slope0_ref[at, lanes]
            dn_ref[at, lanes] = dnorm
            one = one + dnorm
            two = two + dnorm * norm_ref[at, lanes]
        return one, two

    one, two = lax.fori_loop(0, rows // STEP, back, (zero, zero))
    local_one = jnp.sum(one, 0, keepdims=True)
    local_two = jnp.sum(two, 0, keepdims=True)
    stat_ref[1, 0:1, :] = local_one
    stat_ref[1, 1:2, :] = local_two
    copies = share(1)
    for part in (0, 1, 2):
        advance(part)
    total = gathered(1, copies)
    mean_one, mean_two = total[0:1] / count, total[1:2] / count
    scale = gain * inverse

    def through_norm(i, carry):
        at = pl.ds(pl.multiple_of(i * STEP, STEP), STEP)
        for q in range(4):
            lanes = slice(q * C, (q + 1) * C)
            dn_ref[at, lanes] = scale * (dn_ref[at, lanes] - mean_one - norm_ref[at, lanes] * mean_two)
        return carry

    lax.fori_loop(0, rows // STEP, through_norm, 0)
    for part in (3, 4, 5):
        advance(part)
    grad_zero = jnp.zeros((32, C), F32)
    for q in range(4):
        taps = dot(xx_ref[:rows, :32], dn_ref[:, q * C : (q + 1) * C], 0, 0, HIGH)
        grad_zero = grad_zero + (taps if q == 0 else pltpu.roll(taps, 32 - 5 * q, 0))
    little[0] = grad_zero[:16]
    little[0, 10:11, :] = local_two
    little[0, 11:12, :] = local_one

    small_copies = []

    def launch_small():
        step = len(small_copies)
        copy = pltpu.make_async_remote_copy(
            src_ref=little.at[step],
            dst_ref=little_in.at[step],
            send_sem=sm_send.at[step],
            recv_sem=sm_recv.at[step],
            device_id=partner(orders[0][step]),
            device_id_type=MESH,
        )
        copy.start()
        small_copies.append(copy)

    def absorb_small():
        step = len(small_copies) - 1
        small_copies[-1].wait_recv()
        little[step + 1] = little[step] + little_in[step]

    launch_small()
    while min(s["step"] for s in state) <= 2 * stages:
        for part in (3, 4, 5, 0, 1, 2):
            if state[part]["step"] <= 2 * stages:
                advance(part)
        if len(small_copies) < stages:
            absorb_small()
            launch_small()
    while len(small_copies) < stages:
        absorb_small()
        launch_small()
    absorb_small()
    small_ref[...] = little[stages]
    for s in state:
        for copy in s["back"]:
            copy.wait_send()
        for copy, _, _, _, whole in s["sent"]:
            if not whole:
                copy.wait_send()
    for copy in small_copies:
        copy.wait_send()


def shards(tm, rec, audio, conv0_weight, norm_gain, norm_bias, conv1_weight, conv2_weight, cotangent):
    samples = audio.shape[1]
    rows = samples // 20
    rows_all = rows + EDGE
    C = conv0_weight.shape[1]
    lines = jnp.pad(audio.reshape(rows, 20), ((0, 0), (0, 108)))
    taps = jnp.concatenate([conv0_weight, jnp.zeros((22, C), F32)], 0)
    stages = (tm.bit_length() - 1) + (rec.bit_length() - 1)
    total_rows = 6 * C
    vmem = pl.BlockSpec(memory_space=pltpu.VMEM)
    features, res, small = pl.pallas_call(
        functools.partial(kernel, tm, rec),
        out_shape=(
            jax.ShapeDtypeStruct((rows, C), BF16),
            jax.ShapeDtypeStruct((total_rows, C), BF16),
            jax.ShapeDtypeStruct((16, C), F32),
        ),
        in_specs=[vmem] * 4 + [pl.BlockSpec(memory_space=pltpu.HBM)] * 2 + [vmem],
        out_specs=(vmem,) * 3,
        scratch_shapes=[
            pltpu.VMEM((rows_all, 4 * C), F32),
            pltpu.VMEM((rows_all, 4 * C), F32),
            pltpu.VMEM((rows_all, 5 * C), BF16),
            pltpu.VMEM((rows_all, 2 * C), F32),
            pltpu.VMEM((rows_all, 2 * C), F32),
            pltpu.VMEM((rows_all, 3 * C), BF16),
            pltpu.VMEM((rows_all, C), F32),
            pltpu.VMEM((rows_all, C), BF16),
            pltpu.VMEM((rows_all, 2 * C), BF16),
            pltpu.VMEM((rows_all, 128), F32),
            pltpu.VMEM((rows_all, 128), F32),
            pltpu.VMEM((32, 4 * C), F32),
            pltpu.VMEM((EDGE, C), BF16),
            pltpu.VMEM((rows, 4 * C), F32),
            pltpu.VMEM((rows_all, 3 * C), F32),
            pltpu.VMEM((rows_all, 3 * C), F32),
            pltpu.VMEM((total_rows, C), F32),
            pltpu.VMEM((total_rows, C), BF16),
            pltpu.VMEM((6, total_rows // 6 + 96, C), BF16),
            pltpu.VMEM((2, 2, C), F32),
            pltpu.VMEM((2, tm, 2, C), F32),
            pltpu.VMEM((stages + 1, 16, C), F32),
            pltpu.VMEM((stages, 16, C), F32),
            pltpu.VMEM((3 * C, C), BF16),
            pltpu.VMEM((3 * C, C), BF16),
            pltpu.SemaphoreType.DMA((2,)),
            pltpu.SemaphoreType.DMA((3,)),
            pltpu.SemaphoreType.DMA((3,)),
            pltpu.SemaphoreType.DMA((6, 2 * stages)),
            pltpu.SemaphoreType.DMA((6, 2 * stages)),
            pltpu.SemaphoreType.DMA((2, tm)),
            pltpu.SemaphoreType.DMA((2, tm)),
            pltpu.SemaphoreType.DMA((stages,)),
            pltpu.SemaphoreType.DMA((stages,)),
        ],
        compiler_params=pltpu.CompilerParams(
            collective_id=0, has_side_effects=True, vmem_limit_bytes=52 * 2**20
        ),
    )(lines, taps, norm_gain[None, :], norm_bias[None, :], conv1_weight, conv2_weight, cotangent[0])
    grad_two = res[: 3 * C].astype(F32)
    grad_one = res[3 * C :].astype(F32)
    return (features[None], small[:10], small[10], small[11], grad_one, grad_two)


def solution(mesh):
    return jax.shard_map(
        functools.partial(shards, mesh.shape["tm"], mesh.shape["rec"]),
        mesh=mesh,
        in_specs=(P("rec", "tm"), P(), P(), P(), P(), P(), P("rec", "tm", None)),
        out_specs=(P("rec", "tm", None), P(), P(), P(), P(), P()),
        check_vma=False,
    )
```

profile of v0, /device:TPU:1, one launch (start us, length us, event | category | flops | bytes accessed | tf_op | source)
XLA Modules:
  0.0 74.8 jit_solution(13669889344445556902)
XLA Ops:
  0.6 0.5 broadcast.7
  1.1 1.4 %reduce.3 = f32[5120]{0:T(1024)S(1)} reduce(f32[1,5120]{1,0:T(1,128)} %param.7, f32[]{:T(128)} %broadcast.7), dimensions={0}, to_apply=%param.7.reduce_sub_computation.3 | reduce | bytes 40964 | tf_op args[0]
  2.6 0.8 %concatenate.3.taps_ref = f32[32,512]{1,0:T(8,128)S(1)} pad(f32[10,512]{1,0:T(8,128)} %param.8, f32[]{:T(128)} %constant.1.clone.1), padding=0_22x0_0 | pad | bytes 86020 | tf_op jit(solution)/shard_map/concatenate | solution.py:386
  3.3 0.1 reshape.15
  3.5 0.0 copy-start
  3.5 0.9 %copy-done = bf16[1,256,512]{2,1,0:T(8,128)(2,1)S(1)} copy-done((bf16[1,256,512]{2,1,0:T(8,128)(2,1)S(1)}, bf16[1,256,512]{2,1,0:T(8,128)(2,1)}, u32[]{:S(2)}) %copy-start) | copy-done | bytes 262168
  4.5 0.0 copy-start.1
  4.5 0.7 copy-done.1
  5.1 0.0 copy-start.2
  5.1 0.7 copy-done.2
  5.8 61.6 %shard_map.118 = (bf16[256,512]{1,0:T(8,128)(2,1)S(1)}, bf16[3072,512]{1,0:T(8,128)(2,1)}, f32[16,512]{1,0:T(8,128)S(1)}) custom-call(f32[256,128]{1,0:T(8,128)S(1)} %pad.5.audio_ref, f32[32,512]{1,0:T(8,128)S(1)} %concatenate.3.taps_ref, f32[1,512]{1,0:T(1,128)S(1)} %bitcast.10, f32[1,512]{1,0:T(1,128)S(1)} %bitcast.11, bf16[1536,512]{1,0:T(8,128)(2,1)} %w1_hbm.1, ...), custom_call_target="tpu_custom_call" | custom-call | tf_op jit(solution)/shard_map/pallas_call | solution.py:390
  67.4 0.6 fusion
  68.0 5.5 %slice_convert_fusion = (f32[1536,512]{1,0:T(8,128)}, f32[1536,512]{1,0:T(8,128)}) fusion(bf16[3072,512]{1,0:T(8,128)(2,1)} %get-tuple-element.11), kind=kLoop, calls=%fused_computation | loop fusion | flops 1572864 | bytes 9437184 | tf_op jit(solution)/shard_map/convert_element_type | solution.py:439
  73.5 0.7 copy.15
  74.2 0.6 copy.16
  (1 shorter events, 0.0 us)
Async XLA Ops:
  3.5 1.0 %copy-start = (bf16[1,256,512]{2,1,0:T(8,128)(2,1)S(1)}, bf16[1,256,512]{2,1,0:T(8,128)(2,1)}, u32[]{:S(2)}) copy-start(bf16[1,256,512]{2,1,0:T(8,128)(2,1)} %param.13) | copy-start | bytes 786436
  4.5 0.7 copy-start.1
  5.1 0.7 copy-start.2
where the time goes:
time: 75.1 us; the launch traced here: 74.8 us
  Pallas kernels  61.6 us (82%)
  other arithmetic  6.9 us (9%)
  local copies, waits for them, and re-layouts  5.65 us (8%)
    pallas_call x1, Pallas kernels, shards(): pl.pallas_call(functools.partial(kernel, tm, rec), out_shape=(jax.ShapeDt...  61.6 us
    convert_element_type x1, other arithmetic, shards(): grad_two = res[:3 * C].astype(F32)  5.48 us
    unnamed x9, local copies, waits for them, and re-layouts  4.14 us

commit v1 on v0

v1 whole, which is shorter than its diff:
```python
import functools

import jax
import jax.numpy as jnp
from jax import lax
from jax.experimental import pallas as pl
from jax.experimental.pallas import tpu as pltpu
from jax.sharding import PartitionSpec as P

EPS = 1e-05
HIGH = lax.Precision.HIGHEST
MESH = pl.DeviceIdType.MESH
F32, BF16 = jnp.float32, jnp.bfloat16
EDGE = 16
STEP = 16
PARTS = 6
PLANS = {1: 'zp'}
ORDER = (
    2, 1, 6, 2, 1, 0, 5, 4, 0, 3, 6, 6, 3, 2, 5, 4, 6, 0, 6, 6, 6, 2, 6, 3,
    1, 6, 6, 6, 0, 6, 5, 6, 2, 3, 1, 4, 0, 5, 2, 6, 3, 4, 1, 0, 5, 6, 3, 4,
    5, 1, 4,
)
INFO = 24


def gelu_parts(value):
    phi = 0.5 * (1.0 + lax.erf(value * 0.7071067811865476))
    slope = phi + value * jnp.exp(-0.5 * value * value) * 0.3989422804014327
    return value * phi, slope


def dot(a, b, ca, cb, precision=None):
    return lax.dot_general(
        a, b, (((ca,), (cb,)), ((), ())), precision=precision, preferred_element_type=F32
    )


def axes_of(tm, rec):
    plane = [1 << i for i in range(1, tm.bit_length() - 1)]
    return {"p": ("tm", plane), "z": ("rec", [1 << i for i in range(rec.bit_length() - 1)])}


def plan(tm, rec, rows):
    axes, plans = axes_of(tm, rec), []
    for part in range(PARTS):
        size, stages = rows, []
        for name in PLANS.get(part, "pz"):
            axis, bits = axes[name]
            members = 1 << len(bits)
            whole = size // members < 16 or size % (16 * members) != 0
            size = size if whole else size // members
            stages.append((axis, bits, members, size, whole))
        plans.append(stages)
    return plans


def recv_rows(stages, rows):
    return rows + sum(size * members for _, _, members, size, _ in stages)


def kernel(
    tm, rec, audio_hbm, taps_hbm, gain_hbm, bias_hbm, w1_hbm, w2_hbm, cot_hbm,
    features_ref, res_ref, small_ref,
    audio_ref, taps_ref, gain_ref, bias_ref, cot_ref, gram_ref, lhs_ref, wide_ref, info_ref, info_in,
    norm_ref, slope0_ref, act0_ref, pre1_ref, slope1_ref, act1_ref, pre2_ref, delta2_ref, delta1_ref,
    xx_ref, edge_ref, dn_ref, t0_ref, t1_ref, gf_ref, corebuf, sendbuf, recvbuf, lit_ref, lit_core, lit_xy, lit_z,
    w1_ref, w2_ref, load_sem, ed_send, ed_recv, in_send, in_recv, co_send, co_recv, rs_send, rs_recv, ag_send, ag_recv,
    sm_send, sm_recv,
):
    me = {"tm": lax.axis_index("tm"), "rec": lax.axis_index("rec")}
    rows_all, C = pre2_ref.shape
    H = C // 2
    rows = rows_all - EDGE
    count = 4.0 * rows * tm
    inside = 4.0 * rows - 1.0
    part_rows = gf_ref.shape[1]
    plans = plan(tm, rec, part_rows)
    core = lax.rem(me["tm"], 2)
    sibling = {"tm": me["tm"] + 1 - 2 * core}

    def bit_of(axis, bit):
        return lax.rem(me[axis] // bit, 2)

    def place(axis, bits, mask=0):
        where = 0
        for i, bit in enumerate(bits):
            own = bit_of(axis, bit)
            where = where + ((1 - own) if mask >> i & 1 else own) * (1 << i)
        return where

    def partner(axis, bits, mask):
        index = me[axis]
        for i, bit in enumerate(bits):
            if mask >> i & 1:
                index = index + bit * (1 - 2 * bit_of(axis, bit))
        return {axis: index}

    loads = [
        pltpu.make_async_copy(source, target, load_sem.at[i])
        for i, (source, target) in enumerate((
            (audio_hbm, audio_ref), (taps_hbm, taps_ref), (gain_hbm, gain_ref), (bias_hbm, bias_ref),
            (cot_hbm, cot_ref), (w1_hbm, w1_ref), (w2_hbm, w2_ref),
        ))
    ]
    for load in loads:
        load.start()
    barrier = pltpu.get_barrier_semaphore()
    for d in range(1, tm):
        pl.semaphore_signal(barrier, inc=1, device_id={"tm": lax.rem(me["tm"] + d, tm)}, device_id_type=MESH)
    for d in range(1, rec):
        pl.semaphore_signal(barrier, inc=1, device_id={"rec": lax.rem(me["rec"] + d, rec)}, device_id_type=MESH)

    loads[0].wait()
    groups = rows // 32
    blocks = [audio_ref[pl.ds(k, groups, stride=5), :] for k in range(5)]
    blocks.append(pltpu.roll(blocks[0], groups - 1, 0))
    lane = lax.broadcasted_iota(jnp.int32, (groups, 128), 1)
    for s in range(32):
        k, off = divmod(20 * s, 128)
        piece = blocks[k]
        if off:
            piece = pltpu.roll(piece, 128 - off, 1)
        if off + 25 > 128:
            piece = jnp.where(lane < 128 - off, piece, pltpu.roll(blocks[k + 1], 128 - off, 1))
        xx_ref[pl.ds(s, groups, stride=32), :] = jnp.where(lane < 25, piece, 0.0)
    shift = jnp.sum(jnp.sum(audio_ref[...], 0, keepdims=True), 1, keepdims=True) / (20.0 * rows)
    x = xx_ref[:rows, :]
    lane = lax.broadcasted_iota(jnp.int32, x.shape, 1)
    row = lax.broadcasted_iota(jnp.int32, x.shape, 0)
    level = x - shift
    last = jnp.logical_and(jnp.logical_and(lane >= 32, lane < 42), row < rows - 1)
    level = jnp.where(lane < 20, level, jnp.where(last, pltpu.roll(level, 17, 1), jnp.where(lane == 64, 1.0, 0.0)))
    gram_ref[...] = dot(level, level, 0, 0, HIGH)
    lane16 = lax.broadcasted_iota(jnp.int32, (16, 128), 1)
    gram, column, line = 0.0, 0.0, 0.0
    ones_row = gram_ref[64:65, :]
    for k in (0, 5, 10, 32):
        piece = gram_ref[k : k + 16, :]
        column = column + piece[:, 64:65]
        gram = gram + (pltpu.roll(piece, 128 - k, 1) if k else piece)
        line = line + (pltpu.roll(ones_row, 128 - k, 1) if k else ones_row)
    info_ref[:16, :] = jnp.where(lane16 < 10, gram, jnp.where(lane16 == 10, column, 0.0))
    info_ref[16:17, :] = line
    info_ref[17:18, :] = xx_ref[0:1, :]
    info_ref[18:19, :] = xx_ref[rows - 1 : rows, :]
    info_ref[19:20, :] = jnp.broadcast_to(shift, (1, 128))
    info_ref[20:, :] = jnp.zeros((INFO - 20, 128), F32)
    info_in[0] = info_ref[...]
    loads[4].wait()

    pl.semaphore_wait(barrier, tm - 1 + rec - 1)
    infos = []
    for d in range(1, tm):
        copy = pltpu.make_async_remote_copy(
            src_ref=info_ref, dst_ref=info_in.at[d], send_sem=in_send.at[d], recv_sem=in_recv.at[d],
            device_id={"tm": lax.rem(me["tm"] + d, tm)}, device_id_type=MESH,
        )
        copy.start()
        infos.append(copy)
    edge_copy = pltpu.make_async_remote_copy(
        src_ref=cot_ref.at[rows - 16 : rows, :], dst_ref=edge_ref, send_sem=ed_send, recv_sem=ed_recv,
        device_id={"tm": lax.rem(me["tm"] + 1, tm)}, device_id_type=MESH,
    )
    edge_copy.start()

    loads[1].wait()
    loads[2].wait()
    loads[3].wait()
    taps = taps_ref[...]
    padded = jnp.concatenate([taps, jnp.zeros((22, C), F32)], 0)
    for q in range(4):
        lanes = slice(q * C, (q + 1) * C)
        value = pltpu.roll(padded, 5 * q, 0) if q else padded
        one = value.astype(BF16)
        rest = value - one.astype(F32)
        two = rest.astype(BF16)
        three = (rest - two.astype(F32)).astype(BF16)
        for i, term in enumerate((one, two, one, two, three, one)):
            wide_ref[32 * i : 32 * (i + 1), lanes] = term
        wide_ref[192:, lanes] = jnp.zeros((64, C), BF16)

    def first_conv(begin, end):
        value = xx_ref[begin:end, :]
        one = value.astype(BF16).astype(F32)
        rest = value - one
        two = rest.astype(BF16).astype(F32)
        three = rest - two
        lhs_ref[begin:end, :128] = (
            one + pltpu.roll(one, 32, 1) + pltpu.roll(two, 64, 1) + pltpu.roll(two, 96, 1)
        ).astype(BF16)
        lhs_ref[begin:end, 128:] = (one + pltpu.roll(three, 32, 1)).astype(BF16)
        norm_ref[begin:end, :] = dot(lhs_ref[begin:end, :], wide_ref[...], 1, 0)

    first_conv(0, rows - 16)
    for copy in infos:
        copy.wait_recv()

    center = info_in[0, 19:20, :]
    for d in range(1, tm):
        center = center + info_in[d, 19:20, :]
    center = center / tm
    gram, column, line = 0.0, 0.0, 0.0
    for d in range(tm):
        off = info_in[d, 19:20, :] - center
        piece, own_line = info_in[d, :16, :], info_in[d, 16:17, :]
        own_column = piece[:, 10:11]
        gram = gram + piece + off * (own_column + own_line + inside * off)
        column = column + own_column + inside * off[:, :1]
        line = line + own_line + inside * off
    ends, starts = info_in[:, 18, :], info_in[:, 17, :]
    lane = lax.broadcasted_iota(jnp.int32, ends.shape, 1)
    slot = lax.broadcasted_iota(jnp.int32, ends.shape, 0)
    starts = jnp.where(slot == lax.rem(me["tm"] + 1, tm), 0.0, pltpu.roll(pltpu.roll(starts, 5, 1), 1, 0))
    cross = jnp.where(lane < 5, pltpu.roll(ends, 113, 1), starts) - center
    cross = jnp.where(lane < 10, cross, jnp.where(lane == 10, 1.0, 0.0))
    extra = dot(cross, cross, 0, 0, HIGH)
    gram = gram + extra[:16, :]
    column = (column + extra[:16, 10:11]) / count
    line = (line + extra[10:11, :]) / count
    spread = gram / count - column * line
    taps16 = padded[:16, :]
    through = spread[:, 0:1] * taps[0:1, :]
    for j in range(1, 10):
        through = through + spread[:, j : j + 1] * taps[j : j + 1, :]
    variance = jnp.maximum(jnp.sum(taps16 * through, 0, keepdims=True), 0.0)
    mean = jnp.sum(taps16 * (column + center[:, :1]), 0, keepdims=True)
    inverse = lax.rsqrt(variance + EPS)
    gain, bias = gain_ref[...], bias_ref[...]

    lane = lax.broadcasted_iota(jnp.int32, (16, 128), 1)
    row = lax.broadcasted_iota(jnp.int32, (16, 128), 0)
    after = jnp.where(me["tm"] == tm - 1, 0.0, info_in[tm - 1, 17:18, :])
    before = jnp.where(me["tm"] == 0, 0.0, info_in[1, 18:19, :])
    before = jnp.where(lane[:1] < 20, before, pltpu.roll(info_ref[17:18, :], 20, 1))
    tail = xx_ref[rows - 16 : rows, :]
    fill = jnp.logical_and(row == 15, jnp.logical_and(lane >= 20, lane < 25))
    xx_ref[rows - 16 : rows, :] = jnp.where(fill, pltpu.roll(after, 20, 1), tail)
    xx_ref[rows:, :] = jnp.where(
        lane < 25, jnp.where(row == 0, after, jnp.where(row == 15, before, 0.0)), 0.0
    )
    first_conv(rows - 16, rows_all)

    def first_act(i, carry):
        at = pl.ds(pl.multiple_of(i * STEP, STEP), STEP)
        row = i * STEP + lax.broadcasted_iota(jnp.int32, (STEP, C), 0)
        past = jnp.logical_and(row == rows, me["tm"] == tm - 1)
        for q in range(4):
            lanes = slice(q * C, (q + 1) * C)
            normed = (norm_ref[at, lanes] - mean) * inverse
            norm_ref[at, lanes] = normed
            act, slope = gelu_parts(normed * gain + bias)
            act0_ref[at, lanes] = jnp.where(past, 0.0, act).astype(BF16)
            slope0_ref[at, lanes] = slope
        return carry

    lax.fori_loop(0, rows_all // STEP, first_act, 0)
    act0_ref[:, 4 * C :] = pltpu.roll(act0_ref[:, :C].astype(F32), rows_all - 1, 0).astype(BF16)

    loads[5].wait()
    pre1_ref[:, :C] = dot(act0_ref[:, : 3 * C], w1_ref[...], 1, 0)
    pre1_ref[:, C:] = dot(act0_ref[:, 2 * C :], w1_ref[...], 1, 0)

    def second_act(i, carry):
        at = pl.ds(pl.multiple_of(i * STEP, STEP), STEP)
        row = i * STEP + lax.broadcasted_iota(jnp.int32, (STEP, 2 * C), 0)
        past = jnp.logical_and(row == rows, me["tm"] == tm - 1)
        act, slope = gelu_parts(pre1_ref[at, :])
        act1_ref[at, : 2 * C] = jnp.where(past, 0.0, act).astype(BF16)
        slope1_ref[at, :] = slope
        return carry

    lax.fori_loop(0, rows_all // STEP, second_act, 0)
    act1_ref[:, 2 * C :] = pltpu.roll(act1_ref[:, :C].astype(F32), rows_all - 1, 0).astype(BF16)

    loads[6].wait()
    pre2_ref[...] = dot(act1_ref[...], w2_ref[...], 1, 0)

    def third_act(i, carry):
        at = pl.ds(pl.multiple_of(i * STEP, STEP), STEP)
        act, slope = gelu_parts(pre2_ref[at, :])
        features_ref[at, :] = act.astype(BF16)
        delta2_ref[at, :] = (cot_ref[at, :].astype(F32) * slope).astype(BF16)
        return carry

    lax.fori_loop(0, rows // STEP, third_act, 0)
    edge_copy.wait_recv()
    slope = gelu_parts(pre2_ref[rows:, :])[1]
    edge = jnp.where(me["tm"] == 0, 0.0, edge_ref[...].astype(F32))
    delta2_ref[rows:, :] = (edge * slope).astype(BF16)

    state = [
        {"size": part_rows, "start": 0, "used": part_rows, "step": 0, "wait": [], "sent": [], "bases": [0], "kept": []}
        for _ in range(PARTS)
    ]

    def combine(target, offset, part, start, size, began, bases):
        block = min(32, size)

        def body(i, carry):
            at = pl.ds(pl.multiple_of(start + i * block, 16), block)
            value = gf_ref[part, at, :]
            for base in bases:
                came = pl.ds(pl.multiple_of(base + (start - began) + i * block, 16), block)
                value = value + recvbuf[part, came, :].astype(F32)
            to = pl.ds(pl.multiple_of(offset + start + i * block, 16), block)
            target[to, :] = value.astype(target.dtype)
            return carry

        lax.fori_loop(0, size // block, body, 0)

    def settle(part, start, size, base, members):
        block = min(32, size)

        def body(i, carry):
            value = 0.0
            for slot in range(members):
                came = pl.ds(pl.multiple_of(base + slot * size + i * block, 16), block)
                value = value + recvbuf[part, came, :].astype(F32)
            gf_ref[part, pl.ds(pl.multiple_of(start + i * block, 16), block), :] = value
            return carry

        lax.fori_loop(0, size // block, body, 0)

    def start_core(part, value):
        corebuf[part] = value.astype(BF16)
        copy = pltpu.make_async_remote_copy(
            src_ref=corebuf.at[part], dst_ref=recvbuf.at[part, pl.ds(0, part_rows), :],
            send_sem=co_send.at[part, 0], recv_sem=co_recv.at[part, 0], device_id=sibling, device_id_type=MESH,
        )
        copy.start()
        state[part]["wait"] = [copy]
        state[part]["sent"].append(copy)

    def advance(part):
        s, stages = state[part], plans[part]
        step = s["step"]
        s["step"] += 1
        for copy in s["wait"]:
            copy.wait_recv()
        s["wait"] = []
        size, start = s["size"], s["start"]
        if step <= len(stages) and step > 0 and stages[step - 1][4]:
            settle(part, start, size, s["bases"][0], stages[step - 1][2])
            s["bases"] = []
        if step < len(stages):
            axis, bits, members, out, whole = stages[step]
            here = place(axis, bits)
            base = s["used"]
            for mask in range(1, members):
                there = place(axis, bits, mask)
                if whole:
                    away = start
                    if mask == 1:
                        combine(sendbuf.at[part], 0, part, start, size, start, s["bases"])
                        own = pl.ds(pl.multiple_of(base + here * size, 16), size)
                        recvbuf[part, own, :] = sendbuf[part, pl.ds(pl.multiple_of(start, 16), size), :]
                    to = base + here * size
                else:
                    away = start + there * out
                    combine(sendbuf.at[part], 0, part, away, out, start, s["bases"])
                    to = base + (mask - 1) * out
                copy = pltpu.make_async_remote_copy(
                    src_ref=sendbuf.at[part, pl.ds(pl.multiple_of(away, 16), out), :],
                    dst_ref=recvbuf.at[part, pl.ds(pl.multiple_of(to, 16), out), :],
                    send_sem=rs_send.at[part, step, mask], recv_sem=rs_recv.at[part, step, mask],
                    device_id=partner(axis, bits, mask), device_id_type=MESH,
                )
                copy.start()
                s["wait"].append(copy)
                s["sent"].append(copy)
            if whole:
                s["bases"] = [base]
                s["kept"].append(None)
            else:
                keep = start + here * out
                combine(gf_ref.at[part], 0, part, keep, out, start, s["bases"])
                s["bases"] = [base + i * out for i in range(members - 1)]
                s["kept"].append((keep, out))
                s["start"] = keep
            s["size"], s["used"] = out, base + members * out
            return
        if step == len(stages):
            combine(res_ref.at[core], part * part_rows, part, start, size, start, s["bases"])
        back = 2 * len(stages) - 1 - step
        while back >= 0 and s["kept"][back] is None:
            back -= 1
            s["step"] += 1
        if back >= 0:
            axis, bits, members, _, _ = stages[back]
            keep, out = s["kept"][back]
            piece = res_ref.at[core, pl.ds(pl.multiple_of(part * part_rows + keep, 16), out), :]
            for mask in range(1, members):
                copy = pltpu.make_async_remote_copy(
                    src_ref=piece, dst_ref=piece,
                    send_sem=ag_send.at[part, back, mask], recv_sem=ag_recv.at[part, back, mask],
                    device_id=partner(axis, bits, mask), device_id_type=MESH,
                )
                copy.start()
                s["wait"].append(copy)
                s["sent"].append(copy)
        elif back == -1:
            piece = res_ref.at[core, pl.ds(part * part_rows, part_rows), :]
            copy = pltpu.make_async_remote_copy(
                src_ref=piece, dst_ref=piece, send_sem=co_send.at[part, 1], recv_sem=co_recv.at[part, 1],
                device_id=sibling, device_id_type=MESH,
            )
            copy.start()
            s["wait"].append(copy)
            s["sent"].append(copy)

    mine = pl.ds(pl.multiple_of(core * H, H), H)
    other = pl.ds(pl.multiple_of((1 - core) * H, H), H)
    half = PARTS // 2

    def weight_grad(part, lanes):
        begin = (part % half) * part_rows
        one = slice(begin, begin + part_rows)
        two = slice(2 * C + begin, 2 * C + begin + part_rows)
        if part < half:
            return dot(act1_ref[:rows, one], delta2_ref[:rows, lanes], 0, 0)
        first, second = delta1_ref.at[:rows, :C], delta1_ref.at[:rows, C:]
        return dot(act0_ref[:rows, one], first[:, lanes], 0, 0) + dot(act0_ref[:rows, two], second[:, lanes], 0, 0)

    def advance_part(part):
        step = state[part]["step"]
        if step == 0 and not state[part]["sent"]:
            start_core(part, weight_grad(part, other))
            return
        if step == 0:
            gf_ref[part] = weight_grad(part, mine)
        if step <= 2 * len(plans[part]) + 2:
            advance(part)

    def second_delta():
        t0_ref[...] = dot(delta2_ref[...], w2_ref[...], 1, 1)
        even = t0_ref[:, :C] + pltpu.roll(t0_ref[:, 2 * C :], 1, 0)
        delta1_ref[:, :C] = (even * slope1_ref[:, :C]).astype(BF16)
        delta1_ref[:, C:] = (t0_ref[:, C : 2 * C] * slope1_ref[:, C:]).astype(BF16)

    def even_back():
        t0_ref[...] = dot(delta1_ref[:, :C], w1_ref[...], 1, 1)

    def odd_back():
        t1_ref[...] = dot(delta1_ref[:, C:], w1_ref[...], 1, 1)
        t1_ref[:, 2 * C :] = pltpu.roll(t1_ref[:, 2 * C :], 1, 0)

    zero = jnp.zeros((STEP, C), F32)

    def back(i, carry):
        one, two = carry
        at = pl.ds(pl.multiple_of(i * STEP, STEP), STEP)
        grads = (
            t0_ref[at, :C] + t1_ref[at, 2 * C :],
            t0_ref[at, C : 2 * C],
            t0_ref[at, 2 * C :] + t1_ref[at, :C],
            t1_ref[at, C : 2 * C],
        )
        for q in range(4):
            lanes = slice(q * C, (q + 1) * C)
            dnorm = grads[q] * slope0_ref[at, lanes]
            dn_ref[at, lanes] = dnorm
            one = one + dnorm
            two = two + dnorm * norm_ref[at, lanes]
        return one, two

    sums = {"both": (zero, zero), "taps": jnp.zeros((32, C), F32)}
    quarter = rows // STEP // 4

    def back_rows(i):
        sums["both"] = lax.fori_loop(i * quarter, (i + 1) * quarter, back, sums["both"])

    def taps_of(q):
        samples = xx_ref[:rows, :] - center
        total = dot(samples[:, :32], dn_ref[:, q * C : (q + 1) * C], 0, 0, HIGH)
        sums["taps"] = sums["taps"] + (pltpu.roll(total, 32 - 5 * q, 0) if q else total)

    def small_grads():
        local_one, local_two = (jnp.sum(value, 0, keepdims=True) for value in sums["both"])
        grad_zero = (gain * inverse) * (sums["taps"][:16] - local_one * column - (local_two * inverse) * through)
        row = lax.broadcasted_iota(jnp.int32, (16, C), 0)
        little = jnp.where(row < 10, grad_zero, jnp.where(row == 10, local_two, jnp.where(row == 11, local_one, 0.0)))
        lit_ref[0], lit_ref[1] = little[:, :H], little[:, H:]

    plane, z = (axes_of(tm, rec)[name] for name in "pz")
    small_state = {"wait": [], "sent": [], "step": 0}

    def send_small(source, target, group, device):
        copy = pltpu.make_async_remote_copy(
            src_ref=source, dst_ref=target, send_sem=sm_send.at[group], recv_sem=sm_recv.at[group],
            device_id=device, device_id_type=MESH,
        )
        copy.start()
        small_state["wait"].append(copy)
        small_state["sent"].append(copy)

    def spread_small(buffer, axis, bits, first_sem):
        here = buffer.at[place(axis, bits)]
        for mask in range(1, 1 << len(bits)):
            send_small(here, here, first_sem + mask, partner(axis, bits, mask))

    def total_of(buffer):
        total = buffer[0]
        for i in range(1, buffer.shape[0]):
            total = total + buffer[i]
        return total

    def advance_small():
        step = small_state["step"]
        small_state["step"] += 1
        for copy in small_state["wait"]:
            copy.wait_recv()
        small_state["wait"] = []
        if step == 0:
            send_small(lit_ref.at[1 - core], lit_core, 0, sibling)
        elif step == 1:
            lit_xy[place(*plane)] = lit_ref[core] + lit_core[...]
            spread_small(lit_xy, *plane, 0)
        elif step == 2:
            lit_z[place(*z)] = total_of(lit_xy)
            spread_small(lit_z, *z, lit_xy.shape[0])
        elif step == 3:
            small_ref[core] = total_of(lit_z)
            send_small(small_ref.at[core], small_ref.at[core], lit_xy.shape[0] + lit_z.shape[0], sibling)

    def first_small():
        small_grads()
        advance_small()

    main = [second_delta, even_back, odd_back]
    main += [functools.partial(back_rows, i) for i in range(4)] + [functools.partial(taps_of, q) for q in range(4)]
    main += [first_small] + [advance_small] * 4
    for item in ORDER:
        if item < PARTS:
            advance_part(item)
        elif main:
            main.pop(0)()
    for work in main:
        work()
    while min(s["step"] - 2 * len(p) for s, p in zip(state, plans)) < 3:
        for part in range(PARTS):
            advance_part(part)
    for s in state:
        for copy in s["sent"]:
            copy.wait_send()
    for copy in small_state["sent"] + infos + [edge_copy]:
        copy.wait_send()


def finish(
    features_ref, res_ref, small_ref, features_hbm, zero_hbm, gain_hbm, bias_hbm, one_hbm, two_hbm,
    wide_ref, zero_ref, gain_ref, bias_ref, sem,
):
    H = res_ref.shape[2]
    per = one_hbm.shape[0]
    copies = []

    def send(source, target):
        copy = pltpu.make_async_copy(source, target, sem.at[len(copies)])
        copy.start()
        copies.append(copy)

    send(features_ref, features_hbm)
    for h in range(2):
        lanes = slice(h * H, (h + 1) * H)
        zero_ref[:, lanes] = small_ref[h, :10, :]
        gain_ref[:, lanes] = small_ref[h, 10:11, :]
        bias_ref[:, lanes] = small_ref[h, 11:12, :]
    send(zero_ref, zero_hbm)
    send(gain_ref, gain_hbm)
    send(bias_ref, bias_hbm)
    chunk = per // 4
    for i in range(8):
        at = slice(i * chunk, (i + 1) * chunk)
        for h in range(2):
            wide_ref[at, h * H : (h + 1) * H] = res_ref[h, at, :].astype(F32)
        target = two_hbm if i < 4 else one_hbm
        begin = (i % 4) * chunk
        send(wide_ref.at[at, :], target.at[begin : begin + chunk, :])
    for copy in copies:
        copy.wait()


def shards(tm, rec, audio, conv0_weight, norm_gain, norm_bias, conv1_weight, conv2_weight, cotangent):
    samples = audio.shape[1]
    rows = samples // 20
    rows_all = rows + EDGE
    C = conv0_weight.shape[1]
    H = C // 2
    total_rows = 6 * C
    part_rows = total_rows // PARTS
    plans = plan(tm, rec, part_rows)
    received = max(recv_rows(stages, part_rows) for stages in plans)
    most = max(members for stages in plans for _, _, members, _, _ in stages)
    stages = len(plans[0])
    chips = tm // 2
    vmem = pl.BlockSpec(memory_space=pltpu.VMEM)
    hbm = pl.BlockSpec(memory_space=pltpu.HBM)
    dma = pltpu.SemaphoreType.DMA
    features, res, small = pl.pallas_call(
        functools.partial(kernel, tm, rec),
        out_shape=(
            jax.ShapeDtypeStruct((rows, C), BF16),
            jax.ShapeDtypeStruct((2, total_rows, H), BF16),
            jax.ShapeDtypeStruct((2, 16, H), F32),
        ),
        in_specs=[hbm] * 7,
        out_specs=(vmem,) * 3,
        scratch_shapes=[
            pltpu.VMEM((samples // 128, 128), F32),
            pltpu.VMEM((10, C), F32),
            pltpu.VMEM((1, C), F32),
            pltpu.VMEM((1, C), F32),
            pltpu.VMEM((rows, C), BF16),
            pltpu.VMEM((128, 128), F32),
            pltpu.VMEM((rows_all, 256), BF16),
            pltpu.VMEM((256, 4 * C), BF16),
            pltpu.VMEM((INFO, 128), F32),
            pltpu.VMEM((tm, INFO, 128), F32),
            pltpu.VMEM((rows_all, 4 * C), F32),
            pltpu.VMEM((rows_all, 4 * C), F32),
            pltpu.VMEM((rows_all, 5 * C), BF16),
            pltpu.VMEM((rows_all, 2 * C), F32),
            pltpu.VMEM((rows_all, 2 * C), F32),
            pltpu.VMEM((rows_all, 3 * C), BF16),
            pltpu.VMEM((rows_all, C), F32),
            pltpu.VMEM((rows_all, C), BF16),
            pltpu.VMEM((rows_all, 2 * C), BF16),
            pltpu.VMEM((rows_all, 128), F32),
            pltpu.VMEM((EDGE, C), BF16),
            pltpu.VMEM((rows, 4 * C), F32),
            pltpu.VMEM((rows_all, 3 * C), F32),
            pltpu.VMEM((rows_all, 3 * C), F32),
            pltpu.VMEM((PARTS, part_rows, H), F32),
            pltpu.VMEM((PARTS, part_rows, H), BF16),
            pltpu.VMEM((PARTS, part_rows, H), BF16),
            pltpu.VMEM((PARTS, received, H), BF16),
            pltpu.VMEM((2, 16, H), F32),
            pltpu.VMEM((16, H), F32),
            pltpu.VMEM((chips, 16, H), F32),
            pltpu.VMEM((rec, 16, H), F32),
            pltpu.VMEM((3 * C, C), BF16),
            pltpu.VMEM((3 * C, C), BF16),
            dma((7,)),
            dma,
            dma,
            dma((tm,)),
            dma((tm,)),
            dma((PARTS, 2)),
            dma((PARTS, 2)),
            dma((PARTS, stages, most)),
            dma((PARTS, stages, most)),
            dma((PARTS, stages, most)),
            dma((PARTS, stages, most)),
            dma((chips + rec + 1,)),
            dma((chips + rec + 1,)),
        ],
        compiler_params=pltpu.CompilerParams(
            collective_id=0, has_side_effects=True, vmem_limit_bytes=44 * 2**20
        ),
    )(*(
        pltpu.with_memory_space_constraint(value, pltpu.HBM)
        for value in (
            audio.reshape(samples // 128, 128), conv0_weight, norm_gain[None, :], norm_bias[None, :],
            conv1_weight, conv2_weight, cotangent[0],
        )
    ))
    features, grad_zero, grad_gain, grad_bias, grad_one, grad_two = pl.pallas_call(
        finish,
        out_shape=(
            jax.ShapeDtypeStruct((rows, C), BF16),
            jax.ShapeDtypeStruct((10, C), F32),
            jax.ShapeDtypeStruct((1, C), F32),
            jax.ShapeDtypeStruct((1, C), F32),
            jax.ShapeDtypeStruct((3 * C, C), F32),
            jax.ShapeDtypeStruct((3 * C, C), F32),
        ),
        in_specs=[vmem] * 3,
        out_specs=(hbm,) * 6,
        scratch_shapes=[
            pltpu.VMEM((total_rows, C), F32),
            pltpu.VMEM((10, C), F32),
            pltpu.VMEM((1, C), F32),
            pltpu.VMEM((1, C), F32),
            dma((12,)),
        ],
        compiler_params=pltpu.CompilerParams(vmem_limit_bytes=24 * 2**20),
    )(features, res, small)
    return (features[None], grad_zero, grad_gain[0], grad_bias[0], grad_one, grad_two)


def solution(mesh):
    return jax.shard_map(
        functools.partial(shards, mesh.shape["tm"], mesh.shape["rec"]),
        mesh=mesh,
        in_specs=(P("rec", "tm"), P(), P(), P(), P(), P(), P("rec", "tm", None)),
        out_specs=(P("rec", "tm", None), P(), P(), P(), P(), P()),
        check_vma=False,
    )
```

time: 75.1 us -> 55 us (0.73)
  Pallas kernels: 61.6 us -> 54.2 us
  other arithmetic: 6.9 us -> 0 us
  local copies, waits for them, and re-layouts: 5.65 us -> 0 us
    pallas_call x1, Pallas kernels: 61.6 us -> 51.4 us  [shards(): pl.pallas_call(functools.partial(kernel, tm, rec), out_shape=(jax.ShapeDt...]
    convert_element_type x1 -> x0, other arithmetic: 5.48 us -> none  [shards(): grad_two = res[:3 * C].astype(F32)]
    unnamed x9 -> x0, local copies, waits for them, and re-layouts: 4.14 us -> none
    pallas_call x0 -> x1, Pallas kernels: none -> 2.86 us  [shards(): pl.pallas_call(finish, out_shape=(jax.ShapeDtypeStruct((rows, C), BF16),...]
    unnamed x1 -> x0, other arithmetic: 1.42 us -> none
    concatenate x1 -> x0, local copies, waits for them, and re-layouts: 0.77 us -> none  [shards(): taps = jnp.concatenate([conv0_weight, jnp.zeros((22, C), F32)], 0)]
where the time goes in v1:
time: 55 us; the launch traced here: 54.9 us
  Pallas kernels  54.2 us (99%)
  between operations  0.64 us (1%)
    pallas_call x1, Pallas kernels, shards(): pl.pallas_call(functools.partial(kernel, tm, rec), out_shape=(jax.ShapeDt...  51.4 us
    pallas_call x1, Pallas kernels, shards(): pl.pallas_call(finish, out_shape=(jax.ShapeDtypeStruct((rows, C), BF16),...  2.86 us

profile of v1, /device:TPU:1, one launch (start us, length us, event | category | flops | bytes accessed | tf_op | source)
XLA Modules:
  0.0 54.9 jit_solution(8425839819173459768)
XLA Ops:
  0.6 51.4 %shard_map.118 = (bf16[256,512]{1,0:T(8,128)(2,1)S(1)}, bf16[2,3072,256]{2,1,0:T(8,128)(2,1)S(1)}, f32[2,16,256]{2,1,0:T(8,128)S(1)}) custom-call(f32[40,128]{1,0:T(8,128)} %bitcast.8, f32[10,512]{1,0:T(8,128)} %taps_hbm.1, f32[1,512]{1,0:T(1,128)} %bitcast.9, f32[1,512]{1,0:T(1,128)} %bitcast.10, bf16[1536,512]{1,0:T(8,128)(2,1)} %w1_hbm.1, ...), custom_call_target="tpu_custom_call" | custom-call | tf_op jit(solution)/shard_map/pallas_call | solution.py:599
  52.0 2.9 %shard_map.119 = (bf16[256,512]{1,0:T(8,128)(2,1)}, f32[10,512]{1,0:T(8,128)}, f32[1,512]{1,0:T(1,128)}, f32[1,512]{1,0:T(1,128)}, f32[1536,512]{1,0:T(8,128)}, /*index=5*/f32[1536,512]{1,0:T(8,128)}) custom-call(bf16[256,512]{1,0:T(8,128)(2,1)S(1)} %get-tuple-element.15.features_ref, bf16[2,3072,256]{2,1,0:T(8,128)(2,1)S(1)} %get-tuple-element.16.res_ref, ...), custom_call_target="tpu_custom_call" | custom-call | tf_op jit(solution)/shard_map/pallas_call | solution.py:667

commit v2 on v1

--- a/solution.py
+++ b/solution.py
@@ -14,11 +14,11 @@
 EDGE = 16
 STEP = 16
 PARTS = 6
-PLANS = {1: 'zp'}
+PLANS = {2: 'zp'}
 ORDER = (
-    2, 1, 6, 2, 1, 0, 5, 4, 0, 3, 6, 6, 3, 2, 5, 4, 6, 0, 6, 6, 6, 2, 6, 3,
-    1, 6, 6, 6, 0, 6, 5, 6, 2, 3, 1, 4, 0, 5, 2, 6, 3, 4, 1, 0, 5, 6, 3, 4,
-    5, 1, 4,
+    1, 2, 6, 1, 2, 4, 0, 0, 6, 4, 6, 1, 6, 6, 5, 3, 6, 6, 6, 5, 0, 2, 6, 1,
+    3, 6, 4, 6, 6, 0, 6, 5, 1, 4, 3, 2, 0, 5, 6, 4, 1, 3, 2, 5, 0, 6, 4, 3,
+    5, 2, 3,
 )
 INFO = 24
 
@@ -62,13 +62,13 @@
     tm, rec, audio_hbm, taps_hbm, gain_hbm, bias_hbm, w1_hbm, w2_hbm, cot_hbm,
     features_ref, res_ref, small_ref,
     audio_ref, taps_ref, gain_ref, bias_ref, cot_ref, gram_ref, lhs_ref, wide_ref, info_ref, info_in,
-    norm_ref, slope0_ref, act0_ref, pre1_ref, slope1_ref, act1_ref, pre2_ref, delta2_ref, delta1_ref,
-    xx_ref, edge_ref, dn_ref, t0_ref, t1_ref, gf_ref, corebuf, sendbuf, recvbuf, lit_ref, lit_core, lit_xy, lit_z,
+    norm_ref, phi0_ref, act0_ref, slope1_ref, act1_ref, delta2_ref, delta1_ref,
+    xx_ref, dn_ref, t0_ref, t1_ref, gf_ref, corebuf, sendbuf, recvbuf, lit_ref, lit_core, lit_xy, lit_z,
     w1_ref, w2_ref, load_sem, ed_send, ed_recv, in_send, in_recv, co_send, co_recv, rs_send, rs_recv, ag_send, ag_recv,
     sm_send, sm_recv,
 ):
     me = {"tm": lax.axis_index("tm"), "rec": lax.axis_index("rec")}
-    rows_all, C = pre2_ref.shape
+    rows_all, C = delta2_ref.shape
     H = C // 2
     rows = rows_all - EDGE
     count = 4.0 * rows * tm
@@ -99,16 +99,18 @@
         pltpu.make_async_copy(source, target, load_sem.at[i])
         for i, (source, target) in enumerate((
             (audio_hbm, audio_ref), (taps_hbm, taps_ref), (gain_hbm, gain_ref), (bias_hbm, bias_ref),
-            (cot_hbm, cot_ref), (w1_hbm, w1_ref), (w2_hbm, w2_ref),
+            (cot_hbm, cot_ref.at[:rows, :]), (w1_hbm, w1_ref), (w2_hbm, w2_ref),
         ))
     ]
-    for load in loads:
-        load.start()
+    loads[0].start()
     barrier = pltpu.get_barrier_semaphore()
     for d in range(1, tm):
         pl.semaphore_signal(barrier, inc=1, device_id={"tm": lax.rem(me["tm"] + d, tm)}, device_id_type=MESH)
     for d in range(1, rec):
         pl.semaphore_signal(barrier, inc=1, device_id={"rec": lax.rem(me["rec"] + d, rec)}, device_id_type=MESH)
+
+    for load in loads[1:]:
+        load.start()
 
     loads[0].wait()
     groups = rows // 32
@@ -146,8 +148,6 @@
     info_ref[19:20, :] = jnp.broadcast_to(shift, (1, 128))
     info_ref[20:, :] = jnp.zeros((INFO - 20, 128), F32)
     info_in[0] = info_ref[...]
-    loads[4].wait()
-
     pl.semaphore_wait(barrier, tm - 1 + rec - 1)
     infos = []
     for d in range(1, tm):
@@ -157,8 +157,9 @@
         )
         copy.start()
         infos.append(copy)
+    loads[4].wait()
     edge_copy = pltpu.make_async_remote_copy(
-        src_ref=cot_ref.at[rows - 16 : rows, :], dst_ref=edge_ref, send_sem=ed_send, recv_sem=ed_recv,
+        src_ref=cot_ref.at[rows - 16 : rows, :], dst_ref=cot_ref.at[rows:, :], send_sem=ed_send, recv_sem=ed_recv,
         device_id={"tm": lax.rem(me["tm"] + 1, tm)}, device_id_type=MESH,
     )
     edge_copy.start()
@@ -240,53 +241,62 @@
     )
     first_conv(rows - 16, rows_all)
 
-    def first_act(i, carry):
-        at = pl.ds(pl.multiple_of(i * STEP, STEP), STEP)
-        row = i * STEP + lax.broadcasted_iota(jnp.int32, (STEP, C), 0)
-        past = jnp.logical_and(row == rows, me["tm"] == tm - 1)
+    def first_act(at, q):
+        lanes = slice(q * C, (q + 1) * C)
+        normed = (norm_ref[at, lanes] - mean) * inverse
+        norm_ref[at, lanes] = normed
+        shifted = normed * gain + bias
+        phi = 0.5 * (1.0 + lax.erf(shifted * 0.7071067811865476))
+        act0_ref[at, lanes] = (shifted * phi).astype(BF16)
+        phi0_ref[at, lanes] = phi
+
+    def first_rows(i, carry):
         for q in range(4):
-            lanes = slice(q * C, (q + 1) * C)
-            normed = (norm_ref[at, lanes] - mean) * inverse
-            norm_ref[at, lanes] = normed
-            act, slope = gelu_parts(normed * gain + bias)
-            act0_ref[at, lanes] = jnp.where(past, 0.0, act).astype(BF16)
-            slope0_ref[at, lanes] = slope
+            first_act(pl.ds(pl.multiple_of(i * STEP, STEP), STEP), q)
         return carry
 
-    lax.fori_loop(0, rows_all // STEP, first_act, 0)
+    lax.fori_loop(0, rows_all // STEP, first_rows, 0)
+
+    @pl.when(me["tm"] == tm - 1)
+    def _():
+        row = lax.broadcasted_iota(jnp.int32, (EDGE, 4 * C), 0)
+        act0_ref[rows:, : 4 * C] = jnp.where(row == 0, 0.0, act0_ref[rows:, : 4 * C].astype(F32)).astype(BF16)
+
     act0_ref[:, 4 * C :] = pltpu.roll(act0_ref[:, :C].astype(F32), rows_all - 1, 0).astype(BF16)
 
     loads[5].wait()
-    pre1_ref[:, :C] = dot(act0_ref[:, : 3 * C], w1_ref[...], 1, 0)
-    pre1_ref[:, C:] = dot(act0_ref[:, 2 * C :], w1_ref[...], 1, 0)
-
-    def second_act(i, carry):
-        at = pl.ds(pl.multiple_of(i * STEP, STEP), STEP)
-        row = i * STEP + lax.broadcasted_iota(jnp.int32, (STEP, 2 * C), 0)
-        past = jnp.logical_and(row == rows, me["tm"] == tm - 1)
-        act, slope = gelu_parts(pre1_ref[at, :])
-        act1_ref[at, : 2 * C] = jnp.where(past, 0.0, act).astype(BF16)
-        slope1_ref[at, :] = slope
-        return carry
-
-    lax.fori_loop(0, rows_all // STEP, second_act, 0)
+
+    def second_act(half, block):
+        lanes = slice(half * C + block * H, half * C + (block + 1) * H)
+        value = dot(act0_ref[:, 2 * half * C : (2 * half + 3) * C], w1_ref[:, block * H : (block + 1) * H], 1, 0)
+        act, slope = gelu_parts(value)
+        act1_ref[:, lanes] = act.astype(BF16)
+        slope1_ref[:, lanes] = slope
+
+    second_act(0, 0)
+    second_act(0, 1)
+    second_act(1, 0)
+    second_act(1, 1)
+
+    @pl.when(me["tm"] == tm - 1)
+    def _():
+        row = lax.broadcasted_iota(jnp.int32, (EDGE, 2 * C), 0)
+        act1_ref[rows:, : 2 * C] = jnp.where(row == 0, 0.0, act1_ref[rows:, : 2 * C].astype(F32)).astype(BF16)
+
     act1_ref[:, 2 * C :] = pltpu.roll(act1_ref[:, :C].astype(F32), rows_all - 1, 0).astype(BF16)
 
     loads[6].wait()
-    pre2_ref[...] = dot(act1_ref[...], w2_ref[...], 1, 0)
-
-    def third_act(i, carry):
-        at = pl.ds(pl.multiple_of(i * STEP, STEP), STEP)
-        act, slope = gelu_parts(pre2_ref[at, :])
-        features_ref[at, :] = act.astype(BF16)
-        delta2_ref[at, :] = (cot_ref[at, :].astype(F32) * slope).astype(BF16)
-        return carry
-
-    lax.fori_loop(0, rows // STEP, third_act, 0)
     edge_copy.wait_recv()
-    slope = gelu_parts(pre2_ref[rows:, :])[1]
-    edge = jnp.where(me["tm"] == 0, 0.0, edge_ref[...].astype(F32))
-    delta2_ref[rows:, :] = (edge * slope).astype(BF16)
+
+    @pl.when(me["tm"] == 0)
+    def _():
+        cot_ref[rows:, :] = jnp.zeros((EDGE, C), BF16)
+
+    for block in range(2):
+        lanes = slice(block * H, (block + 1) * H)
+        act, slope = gelu_parts(dot(act1_ref[...], w2_ref[:, lanes], 1, 0))
+        features_ref[:, lanes] = act[:rows].astype(BF16)
+        delta2_ref[:, lanes] = (cot_ref[:, lanes].astype(F32) * slope).astype(BF16)
 
     state = [
         {"size": part_rows, "start": 0, "used": part_rows, "step": 0, "wait": [], "sent": [], "bases": [0], "kept": []}
@@ -346,11 +356,11 @@
             axis, bits, members, out, whole = stages[step]
             here = place(axis, bits)
             base = s["used"]
-            for mask in range(1, members):
+            for mask in range(members - 1, 0, -1):
                 there = place(axis, bits, mask)
                 if whole:
                     away = start
-                    if mask == 1:
+                    if mask == members - 1:
                         combine(sendbuf.at[part], 0, part, start, size, start, s["bases"])
                         own = pl.ds(pl.multiple_of(base + here * size, 16), size)
                         recvbuf[part, own, :] = sendbuf[part, pl.ds(pl.multiple_of(start, 16), size), :]
@@ -389,7 +399,7 @@
             axis, bits, members, _, _ = stages[back]
             keep, out = s["kept"][back]
             piece = res_ref.at[core, pl.ds(pl.multiple_of(part * part_rows + keep, 16), out), :]
-            for mask in range(1, members):
+            for mask in range(members - 1, 0, -1):
                 copy = pltpu.make_async_remote_copy(
                     src_ref=piece, dst_ref=piece,
                     send_sem=ag_send.at[part, back, mask], recv_sem=ag_recv.at[part, back, mask],
@@ -457,10 +467,13 @@
         )
         for q in range(4):
             lanes = slice(q * C, (q + 1) * C)
-            dnorm = grads[q] * slope0_ref[at, lanes]
+            normed = norm_ref[at, lanes]
+            shifted = normed * gain + bias
+            slope = phi0_ref[at, lanes] + shifted * jnp.exp(-0.5 * shifted * shifted) * 0.3989422804014327
+            dnorm = grads[q] * slope
             dn_ref[at, lanes] = dnorm
             one = one + dnorm
-            two = two + dnorm * norm_ref[at, lanes]
+            two = two + dnorm * normed
         return one, two
 
     sums = {"both": (zero, zero), "taps": jnp.zeros((32, C), F32)}
@@ -610,7 +623,7 @@
             pltpu.VMEM((10, C), F32),
             pltpu.VMEM((1, C), F32),
             pltpu.VMEM((1, C), F32),
-            pltpu.VMEM((rows, C), BF16),
+            pltpu.VMEM((rows_all, C), BF16),
             pltpu.VMEM((128, 128), F32),
             pltpu.VMEM((rows_all, 256), BF16),
             pltpu.VMEM((256, 4 * C), BF16),
@@ -620,13 +633,10 @@
             pltpu.VMEM((rows_all, 4 * C), F32),
             pltpu.VMEM((rows_all, 5 * C), BF16),
             pltpu.VMEM((rows_all, 2 * C), F32),
-            pltpu.VMEM((rows_all, 2 * C), F32),
             pltpu.VMEM((rows_all, 3 * C), BF16),
-            pltpu.VMEM((rows_all, C), F32),
             pltpu.VMEM((rows_all, C), BF16),
             pltpu.VMEM((rows_all, 2 * C), BF16),
             pltpu.VMEM((rows_all, 128), F32),
-            pltpu.VMEM((EDGE, C), BF16),
             pltpu.VMEM((rows, 4 * C), F32),
             pltpu.VMEM((rows_all, 3 * C), F32),
             pltpu.VMEM((rows_all, 3 * C), F32),

time: 55 us -> 53.9 us (0.980)
  Pallas kernels: 54.2 us -> 53.1 us
    pallas_call x1, Pallas kernels: 51.4 us -> 50.3 us  [shards(): pl.pallas_call(functools.partial(kernel, tm, rec), out_shape=(jax.ShapeDt...]
where the time goes in v2:
time: 53.9 us; the launch traced here: 53.8 us
  Pallas kernels  53.1 us (99%)
  between operations  0.64 us (1%)
    pallas_call x1, Pallas kernels, shards(): pl.pallas_call(functools.partial(kernel, tm, rec), out_shape=(jax.ShapeDt...  50.3 us
    pallas_call x1, Pallas kernels, shards(): pl.pallas_call(finish, out_shape=(jax.ShapeDtypeStruct((rows, C), BF16),...  2.86 us

profile of v2, /device:TPU:1, one launch (start us, length us, event | category | flops | bytes accessed | tf_op | source)
XLA Modules:
  0.0 53.8 jit_solution(3030371762535198292)
XLA Ops:
  0.6 50.3 %shard_map.118 = (bf16[256,512]{1,0:T(8,128)(2,1)S(1)}, bf16[2,3072,256]{2,1,0:T(8,128)(2,1)S(1)}, f32[2,16,256]{2,1,0:T(8,128)S(1)}) custom-call(f32[40,128]{1,0:T(8,128)} %bitcast.8, f32[10,512]{1,0:T(8,128)} %taps_hbm.1, f32[1,512]{1,0:T(1,128)} %bitcast.9, f32[1,512]{1,0:T(1,128)} %bitcast.10, bf16[1536,512]{1,0:T(8,128)(2,1)} %w1_hbm.1, ...), custom_call_target="tpu_custom_call" | custom-call | tf_op jit(solution)/shard_map/pallas_call | solution.py:612
  50.9 2.9 %shard_map.119 = (bf16[256,512]{1,0:T(8,128)(2,1)}, f32[10,512]{1,0:T(8,128)}, f32[1,512]{1,0:T(1,128)}, f32[1,512]{1,0:T(1,128)}, f32[1536,512]{1,0:T(8,128)}, /*index=5*/f32[1536,512]{1,0:T(8,128)}) custom-call(bf16[256,512]{1,0:T(8,128)(2,1)S(1)} %get-tuple-element.15.features_ref, bf16[2,3072,256]{2,1,0:T(8,128)(2,1)S(1)} %get-tuple-element.16.res_ref, ...), custom_call_target="tpu_custom_call" | custom-call | tf_op jit(solution)/shard_map/pallas_call | solution.py:677

commit v3 on v2

--- a/solution.py
+++ b/solution.py
@@ -62,7 +62,7 @@
     tm, rec, audio_hbm, taps_hbm, gain_hbm, bias_hbm, w1_hbm, w2_hbm, cot_hbm,
     features_ref, res_ref, small_ref,
     audio_ref, taps_ref, gain_ref, bias_ref, cot_ref, gram_ref, lhs_ref, wide_ref, info_ref, info_in,
-    norm_ref, phi0_ref, act0_ref, slope1_ref, act1_ref, delta2_ref, delta1_ref,
+    norm_ref, act0_ref, slope1_ref, act1_ref, delta2_ref, delta1_ref,
     xx_ref, dn_ref, t0_ref, t1_ref, gf_ref, corebuf, sendbuf, recvbuf, lit_ref, lit_core, lit_xy, lit_z,
     w1_ref, w2_ref, load_sem, ed_send, ed_recv, in_send, in_recv, co_send, co_recv, rs_send, rs_recv, ag_send, ag_recv,
     sm_send, sm_recv,
@@ -241,14 +241,12 @@
     )
     first_conv(rows - 16, rows_all)
 
+    scale = gain * inverse
+
     def first_act(at, q):
         lanes = slice(q * C, (q + 1) * C)
-        normed = (norm_ref[at, lanes] - mean) * inverse
-        norm_ref[at, lanes] = normed
-        shifted = normed * gain + bias
-        phi = 0.5 * (1.0 + lax.erf(shifted * 0.7071067811865476))
-        act0_ref[at, lanes] = (shifted * phi).astype(BF16)
-        phi0_ref[at, lanes] = phi
+        shifted = (norm_ref[at, lanes] - mean) * scale + bias
+        act0_ref[at, lanes] = (shifted * (0.5 * (1.0 + lax.erf(shifted * 0.7071067811865476)))).astype(BF16)
 
     def first_rows(i, carry):
         for q in range(4):
@@ -292,11 +290,17 @@
     def _():
         cot_ref[rows:, :] = jnp.zeros((EDGE, C), BF16)
 
-    for block in range(2):
-        lanes = slice(block * H, (block + 1) * H)
-        act, slope = gelu_parts(dot(act1_ref[...], w2_ref[:, lanes], 1, 0))
+    mine = pl.ds(pl.multiple_of(core * H, H), H)
+    other = pl.ds(pl.multiple_of((1 - core) * H, H), H)
+
+    def third_act(lanes, value):
+        act, slope = gelu_parts(value)
         features_ref[:, lanes] = act[:rows].astype(BF16)
         delta2_ref[:, lanes] = (cot_ref[:, lanes].astype(F32) * slope).astype(BF16)
+
+    theirs = dot(act1_ref[...], w2_ref[:, other], 1, 0)
+    own = dot(act1_ref[...], w2_ref[:, mine], 1, 0)
+    third_act(other, theirs)
 
     state = [
         {"size": part_rows, "start": 0, "used": part_rows, "step": 0, "wait": [], "sent": [], "bases": [0], "kept": []}
@@ -418,8 +422,6 @@
             s["wait"].append(copy)
             s["sent"].append(copy)
 
-    mine = pl.ds(pl.multiple_of(core * H, H), H)
-    other = pl.ds(pl.multiple_of((1 - core) * H, H), H)
     half = PARTS // 2
 
     def weight_grad(part, lanes):
@@ -467,10 +469,8 @@
         )
         for q in range(4):
             lanes = slice(q * C, (q + 1) * C)
-            normed = norm_ref[at, lanes]
-            shifted = normed * gain + bias
-            slope = phi0_ref[at, lanes] + shifted * jnp.exp(-0.5 * shifted * shifted) * 0.3989422804014327
-            dnorm = grads[q] * slope
+            normed = (norm_ref[at, lanes] - mean) * inverse
+            dnorm = grads[q] * gelu_parts(normed * gain + bias)[1]
             dn_ref[at, lanes] = dnorm
             one = one + dnorm
             two = two + dnorm * normed
@@ -489,7 +489,7 @@
 
     def small_grads():
         local_one, local_two = (jnp.sum(value, 0, keepdims=True) for value in sums["both"])
-        grad_zero = (gain * inverse) * (sums["taps"][:16] - local_one * column - (local_two * inverse) * through)
+        grad_zero = scale * (sums["taps"][:16] - local_one * column - (local_two * inverse) * through)
         row = lax.broadcasted_iota(jnp.int32, (16, C), 0)
         little = jnp.where(row < 10, grad_zero, jnp.where(row == 10, local_two, jnp.where(row == 11, local_one, 0.0)))
         lit_ref[0], lit_ref[1] = little[:, :H], little[:, H:]
@@ -542,7 +542,11 @@
     main = [second_delta, even_back, odd_back]
     main += [functools.partial(back_rows, i) for i in range(4)] + [functools.partial(taps_of, q) for q in range(4)]
     main += [first_small] + [advance_small] * 4
-    for item in ORDER:
+    early = next(i for i, item in enumerate(ORDER) if item >= half or item in ORDER[:i])
+    for item in ORDER[:early]:
+        advance_part(item)
+    third_act(mine, own)
+    for item in ORDER[early:]:
         if item < PARTS:
             advance_part(item)
         elif main:
@@ -629,7 +633,6 @@
             pltpu.VMEM((256, 4 * C), BF16),
             pltpu.VMEM((INFO, 128), F32),
             pltpu.VMEM((tm, INFO, 128), F32),
-            pltpu.VMEM((rows_all, 4 * C), F32),
             pltpu.VMEM((rows_all, 4 * C), F32),
             pltpu.VMEM((rows_all, 5 * C), BF16),
             pltpu.VMEM((rows_all, 2 * C), F32),

time: 53.9 us -> 53.7 us (level)
  no operation moved by 1% of the time
where the time goes in v3:
time: 53.7 us; the launch traced here: 53.5 us
  Pallas kernels  52.9 us (99%)
  between operations  0.64 us (1%)
    pallas_call x1, Pallas kernels, shards(): pl.pallas_call(functools.partial(kernel, tm, rec), out_shape=(jax.ShapeDt...  50 us
    pallas_call x1, Pallas kernels, shards(): pl.pallas_call(finish, out_shape=(jax.ShapeDtypeStruct((rows, C), BF16),...  2.86 us

profile of v3, /device:TPU:1, one launch (start us, length us, event | category | flops | bytes accessed | tf_op | source)
XLA Modules:
  0.0 53.5 jit_solution(2649051490320765432)
XLA Ops:
  0.6 50.0 %shard_map.118 = (bf16[256,512]{1,0:T(8,128)(2,1)S(1)}, bf16[2,3072,256]{2,1,0:T(8,128)(2,1)S(1)}, f32[2,16,256]{2,1,0:T(8,128)S(1)}) custom-call(f32[40,128]{1,0:T(8,128)} %bitcast.8, f32[10,512]{1,0:T(8,128)} %taps_hbm.1, f32[1,512]{1,0:T(1,128)} %bitcast.9, f32[1,512]{1,0:T(1,128)} %bitcast.10, bf16[1536,512]{1,0:T(8,128)(2,1)} %w1_hbm.1, ...), custom_call_target="tpu_custom_call" | custom-call | tf_op jit(solution)/shard_map/pallas_call | solution.py:616
  50.7 2.9 %shard_map.119 = (bf16[256,512]{1,0:T(8,128)(2,1)}, f32[10,512]{1,0:T(8,128)}, f32[1,512]{1,0:T(1,128)}, f32[1,512]{1,0:T(1,128)}, f32[1536,512]{1,0:T(8,128)}, /*index=5*/f32[1536,512]{1,0:T(8,128)}) custom-call(bf16[256,512]{1,0:T(8,128)(2,1)S(1)} %get-tuple-element.15.features_ref, bf16[2,3072,256]{2,1,0:T(8,128)(2,1)S(1)} %get-tuple-element.16.res_ref, ...), custom_call_target="tpu_custom_call" | custom-call | tf_op jit(solution)/shard_map/pallas_call | solution.py:680

commit v4 on v3

--- a/solution.py
+++ b/solution.py
@@ -253,7 +253,7 @@
             first_act(pl.ds(pl.multiple_of(i * STEP, STEP), STEP), q)
         return carry
 
-    lax.fori_loop(0, rows_all // STEP, first_rows, 0)
+    lax.fori_loop(0, rows_all // STEP, first_rows, 0, unroll=True)
 
     @pl.when(me["tm"] == tm - 1)
     def _():

time: 53.7 us -> 53.5 us (level)
  no operation moved by 1% of the time
where the time goes in v4:
time: 53.5 us; the launch traced here: 53.4 us
  Pallas kernels  52.7 us (99%)
  between operations  0.64 us (1%)
    pallas_call x1, Pallas kernels, shards(): pl.pallas_call(functools.partial(kernel, tm, rec), out_shape=(jax.ShapeDt...  49.9 us
    pallas_call x1, Pallas kernels, shards(): pl.pallas_call(finish, out_shape=(jax.ShapeDtypeStruct((rows, C), BF16),...  2.86 us

profile of v4, /device:TPU:1, one launch (start us, length us, event | category | flops | bytes accessed | tf_op | source)
XLA Modules:
  0.0 53.4 jit_solution(10696107004735327956)
XLA Ops:
  0.6 49.9 %shard_map.118 = (bf16[256,512]{1,0:T(8,128)(2,1)S(1)}, bf16[2,3072,256]{2,1,0:T(8,128)(2,1)S(1)}, f32[2,16,256]{2,1,0:T(8,128)S(1)}) custom-call(f32[40,128]{1,0:T(8,128)} %bitcast.8, f32[10,512]{1,0:T(8,128)} %taps_hbm.1, f32[1,512]{1,0:T(1,128)} %bitcast.9, f32[1,512]{1,0:T(1,128)} %bitcast.10, bf16[1536,512]{1,0:T(8,128)(2,1)} %w1_hbm.1, ...), custom_call_target="tpu_custom_call" | custom-call | tf_op jit(solution)/shard_map/pallas_call | solution.py:616
  50.5 2.9 %shard_map.119 = (bf16[256,512]{1,0:T(8,128)(2,1)}, f32[10,512]{1,0:T(8,128)}, f32[1,512]{1,0:T(1,128)}, f32[1,512]{1,0:T(1,128)}, f32[1536,512]{1,0:T(8,128)}, /*index=5*/f32[1536,512]{1,0:T(8,128)}) custom-call(bf16[256,512]{1,0:T(8,128)(2,1)S(1)} %get-tuple-element.15.features_ref, bf16[2,3072,256]{2,1,0:T(8,128)(2,1)S(1)} %get-tuple-element.16.res_ref, ...), custom_call_target="tpu_custom_call" | custom-call | tf_op jit(solution)/shard_map/pallas_call | solution.py:680
